TPU v7x, 32 devices: a whole 2x2x4 slice. The times are simulated.
32 devices in a mesh: arc: 4 (over z), tile: 8 (over y, x, core).
Axes of the slice: x: 2, y: 2, z: 4, core: 2. Of those that a mesh axis runs over, the one named last changes fastest.
Arguments:
- design: bfloat16 [256, 128, 512], P(('arc', 'tile')), may hold values from -0.059814453 to 0.059814453
- observed: float32 [256, 128], P(('arc', 'tile')), may hold values from -6 to 6
- obs_type: int32 [256, 128], P(('arc', 'tile')), may hold values from 0 to 7
- owner_of: int32 [256, 4], P(('arc', 'tile')), may hold values from 0 to 7, all different within a row; in each aligned block of 8 rows (0 to 7, 8 to 15, ...) at most 8 rows name the same one
- sub_of: int32 [256, 4], P(('arc', 'tile')), may hold values from 0 to 11
- sigma_table: float32 [8], replicated, may hold values from 0.3 to 3
- solution: float32 [12288], P('tile'), may hold values from -6 to 6
- prior: float32 [12288, 12288], P('arc', 'tile'), may hold values from -0.6 to 0.6
Outputs:
- normal_matrix: float32 [12288, 12288], P('arc', 'tile')
- gradient: float32 [12288], P('tile')
Inputs may be any that keep to these rules, and one draw needn't show every extreme that they name: `owner_of`: each block names 4 different owners. Among the 8 blocks of one device no owner is named more than 8 times, a bound that some block reaches in every draw.
All inputs are finite; a program needn't handle non-finite values.
Results may differ from a plain program's by a relative error of at most 0.006.
Values may be sent and summed in bfloat16 or wider, within the bound.
A program may use at most 256 MiB of HBM per device.

v0:
```python
import jax
import jax.numpy as jnp
from jax import lax
from jax.sharding import PartitionSpec as P

huber_limit = 1.345


def route_table(owner_ids, target_ids, capacity):
    matched = (owner_ids == target_ids[:, None, None]).astype(jnp.int32)
    hit_count = jnp.sum(matched, axis=2)
    slot_pos = jnp.sum(matched * jnp.arange(owner_ids.shape[2], dtype=jnp.int32), axis=2)
    slot_rank = jnp.cumsum(hit_count, axis=1) - 1
    slot_ids = jnp.arange(capacity, dtype=jnp.int32)
    chosen = hit_count[:, None, :] * (slot_rank[:, None, :] == slot_ids[None, :, None]).astype(
        jnp.int32
    )
    live_slot = jnp.sum(chosen, axis=2)
    block_of = jnp.sum(chosen * jnp.arange(owner_ids.shape[1], dtype=jnp.int32), axis=2)
    slot_k = jnp.take_along_axis(slot_pos, block_of, axis=1)
    return (live_slot, block_of, slot_k)


def on_device(design, observed, obs_type, owner_of, sub_of, sigma_table, solution, prior):
    n_owner = lax.axis_size("tile")
    blocks, block_rows, row_width = design.shape
    tile_width = row_width // 4
    params = solution.shape[0] * n_owner
    tile_count = params // tile_width
    per_owner = tile_count // n_owner
    capacity = 2 * ((4 * blocks + n_owner - 1) // n_owner)
    item_count = n_owner * capacity
    own_index = lax.axis_index("tile")
    whole_solution = lax.all_gather(solution, "tile", axis=0, tiled=True)
    tile_ids = owner_of * per_owner + sub_of
    touched = whole_solution.reshape(tile_count, tile_width)[tile_ids]
    design_tiles = design.reshape(blocks, block_rows, 4, tile_width)
    predicted = jnp.einsum(
        "bqlc,blc->bq", design_tiles.astype(jnp.float32), touched, precision=lax.Precision.HIGHEST
    )
    residual = observed - predicted
    type_ids = jnp.arange(sigma_table.shape[0], dtype=jnp.int32)
    spread = jnp.sum(jnp.where(obs_type[:, :, None] == type_ids, sigma_table, 0.0), axis=2)
    scaled = jnp.abs(residual) / spread
    root_weight = jnp.sqrt(huber_limit / jnp.maximum(scaled, huber_limit)) / spread
    weighted = (root_weight[:, :, None, None] * design_tiles).astype(jnp.bfloat16)
    target = (root_weight * residual).astype(jnp.bfloat16)
    owner_copies = jnp.broadcast_to(owner_of[None], (n_owner, blocks, 4))
    send_live, send_block, send_k = route_table(
        owner_copies, jnp.arange(n_owner, dtype=jnp.int32), capacity
    )
    all_owner, all_sub = (
        lax.all_gather(owner_of, "tile", axis=0, tiled=True),
        lax.all_gather(sub_of, "tile", axis=0, tiled=True),
    )
    all_owner = all_owner.reshape(n_owner, blocks, 4)
    all_sub = all_sub.reshape(n_owner, blocks, 4)
    recv_live, recv_block, recv_k = route_table(
        all_owner, jnp.full((n_owner,), own_index, jnp.int32), capacity
    )
    block_pick = jnp.broadcast_to(recv_block[:, :, None], (n_owner, capacity, 4))
    col_tiles = jnp.take_along_axis(all_owner * per_owner + all_sub, block_pick, axis=1)
    sub_rows = jnp.take_along_axis(all_sub, block_pick, axis=1)
    row_sub = jnp.take_along_axis(sub_rows, recv_k[:, :, None], axis=2)[:, :, 0]
    live_flag = send_live > 0
    send_rows = jnp.where(
        live_flag[:, :, None, None],
        weighted.reshape(blocks, block_rows, row_width)[send_block],
        jnp.zeros((), jnp.bfloat16),
    )
    send_target = jnp.where(live_flag[:, :, None], target[send_block], jnp.zeros((), jnp.bfloat16))
    got_rows, got_target = (
        lax.all_to_all(send_rows, "tile", split_axis=0, concat_axis=0, tiled=True),
        lax.all_to_all(send_target, "tile", split_axis=0, concat_axis=0, tiled=True),
    )
    item_rows = got_rows.reshape(item_count, block_rows, 4, tile_width)
    row_pick = (
        recv_k.reshape(item_count)[:, None] == jnp.arange(4, dtype=jnp.int32)[None, :]
    ).astype(jnp.bfloat16)
    row_part = jnp.einsum(
        "iqlc,il->iqc", item_rows, row_pick, preferred_element_type=jnp.float32
    ).astype(jnp.bfloat16)
    item_prod = jnp.einsum(
        "iqlc,iqr->ilcr", item_rows, row_part, preferred_element_type=jnp.float32
    )
    item_pull = jnp.einsum(
        "iqr,iq->ir",
        row_part,
        got_target.reshape(item_count, block_rows),
        preferred_element_type=jnp.float32,
    )
    col_flat = col_tiles.reshape(item_count, 4)
    sub_flat = row_sub.reshape(item_count)
    gram_panel = jnp.zeros((tile_count, tile_width, per_owner, tile_width), jnp.float32)
    gram_panel = gram_panel.at[col_flat, :, sub_flat[:, None], :].add(item_prod)
    grad_part = jnp.zeros((per_owner, tile_width), jnp.float32).at[sub_flat].add(item_pull)
    summed = lax.psum_scatter(
        gram_panel.reshape(params, per_owner * tile_width).astype(jnp.bfloat16),
        "arc",
        scatter_dimension=0,
        tiled=True,
    ).astype(jnp.float32)
    gradient = lax.psum(grad_part.reshape(per_owner * tile_width), "arc")
    return (prior + summed, gradient)


def solution(mesh):
    in_specs = (
        P(("arc", "tile"), None, None),
        P(("arc", "tile"), None),
        P(("arc", "tile"), None),
        P(("arc", "tile"), None),
        P(("arc", "tile"), None),
        P(),
        P("tile"),
        P("arc", "tile"),
    )
    out_specs = (P("arc", "tile"), P("tile"))
    return jax.shard_map(
        on_device, mesh=mesh, in_specs=in_specs, out_specs=out_specs, check_vma=False
    )
```

profile of v0, /device:TPU:0, one launch (start us, length us, event | category | flops | bytes accessed | tf_op | source)
XLA Modules:
  0.0 1055.0 jit_solution(18058328657301075175)
XLA Ops:
  10.8 10.6 %all-gather.2 = f32[8,1,1536]{2,1,0:T(1,128)S(1)} all-gather(f32[1,1,1536]{2,1,0:T(1,128)S(1)} %reshape.413), channel_id=1, replica_groups=mesh['arc'=4,'tile'=8] {'tile'}, dimensions={0}, use_global_device_ids=true | all-gather | bytes 55296 | tf_op jit(solution)/shard_map/all_gather | solution.py:34
  27.0 5.6 gather_fusion.1
  32.6 11.4 %copy.35 = bf16[8,8,128,512]{2,3,1,0:T(8,128)(2,1)} copy(bf16[8,8,128,512]{3,2,1,0:T(8,128)(2,1)} %bitcast.91) | data formatting | bytes 16777216 | tf_op jit(solution)/shard_map/gather | solution.py:68
  44.6 7.4 broadcast_select_fusion
  52.0 5.1 all-to-all-start
  57.1 97.0 %all-gather = s32[8,8,4]{1,2,0:T(4,128)S(1)} all-gather(s32[1,8,4]{1,2,0:T(4,128)S(1)} %bitcast.100), channel_id=1, replica_groups=mesh['arc'=4,'tile'=8] {'tile'}, dimensions={0}, use_global_device_ids=true | all-gather | bytes 1152 | tf_op jit(solution)/shard_map/all_gather | solution.py:53
  155.0 8.2 all-gather.1
  163.2 2.7 gather_fusion.6
  167.2 2.7 gather_fusion.5
  171.3 13.6 %copy.42 = bf16[64,128,4,128]{3,2,1,0:T(4,128)(2,1)} copy(bf16[64,128,4,128]{1,3,2,0:T(8,128)(2,1)} %bitcast.17) | data formatting | bytes 16777216 | tf_op jit(solution)/shard_map/reshape | solution.py:76
  184.9 6.9 fusion.5
  191.8 13.4 %fusion = f32[64,4,128,128]{3,2,1,0:T(8,128)} fusion(bf16[64,128,4,128]{1,3,2,0:T(8,128)(2,1)} %bitcast.17, f32[64,128,128]{2,1,0:T(8,128)S(1)} %bitcast.92), kind=kOutput, calls=%fused_computation.12 | convolution fusion | flops 1074790400 | bytes 29360128 | tf_op jit(solution)/shard_map/iqlc,iqr->ilcr/dot_general | solution.py:83
  205.2 23.9 %broadcast_in_dim.57 = f32[96,128,12,128]{3,1,2,0:T(8,128)} broadcast(f32[]{:T(128)} %constant.26.clone.1), dimensions={} | broadcast | bytes 75497472 | tf_op jit(solution)/shard_map/broadcast_in_dim | solution.py:94
  229.1 52.8 %scatter_fusion = f32[96,128,12,128]{3,1,2,0:T(8,128)} fusion(f32[96,128,12,128]{3,1,2,0:T(8,128)} %broadcast_in_dim.57, s32[256]{0:T(256)S(1)} %reshape.375, f32[256,128,128]{2,1,0:T(8,128)} %bitcast.90), kind=kCustom, calls=%fused_computation.7 | custom fusion | flops 4194304 | bytes 50333696 | tf_op jit(solution)/shard_map/scatter-add | solution.py:95
  281.9 36.4 %convert_element_type.39 = bf16[96,128,12,128]{3,1,2,0:T(8,128)(2,1)} convert(f32[96,128,12,128]{3,1,2,0:T(8,128)} %scatter_fusion) | non-fusion elementwise | flops 18874368 | bytes 113246208 | tf_op jit(solution)/shard_map/convert_element_type | solution.py:98
  318.3 46.2 %copy.36 = bf16[96,128,12,128]{1,0,3,2:T(8,128)(2,1)} copy(bf16[96,128,12,128]{3,1,2,0:T(8,128)(2,1)} %convert_element_type.39) | data formatting | bytes 75497472 | tf_op jit(solution)/shard_map/convert_element_type | solution.py:98
  364.5 26.3 %copy.56 = bf16[192,8,96,128]{3,1,2,0:T(8,128)(2,1)} copy(bf16[192,8,96,128]{3,2,1,0:T(8,128)(2,1)} %bitcast.89) | data formatting | bytes 75497472
  392.8 3.8 all-to-all-start.1
  396.7 18.8 %copy.37 = f32[3072,1536]{0,1:T(8,128)} copy(f32[3072,1536]{1,0:T(8,128)} %param.17) | data formatting | bytes 37748736 | tf_op args[7]
  415.5 2.8 fusion.2
  419.2 13.4 %psum.7 = f32[1536]{0:T(1024)} all-reduce(f32[1536]{0:T(1024)S(1)} %bitcast.99), channel_id=1, replica_groups=mesh['arc'=4,'tile'=8] {'arc'}, use_global_device_ids=true, to_apply=%region_12.14 | all-reduce | flops 1536 | bytes 12288 | tf_op jit(solution)/shard_map/psum | solution.py:103
  432.6 579.5 %reduce-scatter.2.cloned.1.call-done = bf16[3072,1536]{0,1:T(8,128)(2,1)} async-done(((bf16[12288,1536]{0,1:T(8,128)(2,1)}), bf16[3072,1536]{0,1:T(8,128)(2,1)}) %reduce-scatter.2.cloned.1.call-update) | async-done | bytes 9437200 | tf_op jit(solution)/shard_map/reduce_scatter | solution.py:97
  1012.1 17.4 %convert_add_fusion = f32[3072,1536]{0,1:T(8,128)} fusion(f32[3072,1536]{0,1:T(8,128)} %copy.37, bf16[3072,1536]{0,1:T(8,128)(2,1)} %reduce-scatter.2.cloned.1.call-done), kind=kLoop, calls=%fused_computation.10 | loop fusion | flops 9437184 | bytes 47185920 | tf_op jit(solution)/shard_map/add | solution.py:104
  1029.5 18.6 %copy.38 = f32[3072,1536]{1,0:T(8,128)} copy(f32[3072,1536]{0,1:T(8,128)} %convert_add_fusion) | data formatting | bytes 37748736
  (77 shorter events, 16.2 us)
Async XLA Ops:
  8.5 24.1 %copy-start.2 = (s32[1024]{0:T(1024)}, s32[1024]{0:T(1024)S(1)}, u32[]{:S(2)}) copy-start(s32[1024]{0:T(1024)S(1)} %pad_clamp_fusion) | copy-start | bytes 12292
  44.0 0.6 copy-start.5
  52.0 5.2 copy-start.4
  52.0 103.0 %copy-start.7 = (s32[8,4]{0,1:T(4,128)S(1)}, s32[8,4]{0,1:T(4,128)}, u32[]{:S(2)}) copy-start(s32[8,4]{0,1:T(4,128)} %param.14) | copy-start | bytes 388
  52.0 119.4 %all-to-all-start = ((bf16[8,8,128,512]{2,3,1,0:T(8,128)(2,1)}), bf16[8,8,128,512]{2,3,1,0:T(8,128)(2,1)}, u32[]{:S(2)}, u32[]{:S(2)}) async-start(bf16[8,8,128,512]{2,3,1,0:T(8,128)(2,1)} %broadcast_select_fusion), calls=%async_computation | async-start | bytes 16777216 | tf_op jit(solution)/shard_map/all_to_all | solution.py:73
  57.1 955.0 %reduce-scatter.2.cloned.1.call-start = ((), (), s32[]{:S(2)}) async-start(), calls=%async_computation.3 | async-start | bytes 47185920 | tf_op jit(solution)/shard_map/reduce_scatter | solution.py:97
  191.8 13.4 %copy-start = (f32[64,1,128,128]{3,1,2,0:T(1,128)}, f32[64,1,128,128]{3,1,2,0:T(1,128)S(1)}, u32[]{:S(2)}) copy-start(f32[64,1,128,128]{3,1,2,0:T(1,128)S(1)} %fusion.5) | copy-start | bytes 12582916
  390.8 0.7 copy-start.1
  390.8 0.7 copy-start.3
  390.8 1.3 copy-start.6
  392.8 22.7 %all-to-all-start.1 = ((bf16[8,8,128]{2,1,0:T(8,128)(2,1)}), bf16[8,8,128]{2,1,0:T(8,128)(2,1)S(1)}, u32[]{:S(2)}, u32[]{:S(2)}) async-start(bf16[8,8,128]{2,1,0:T(8,128)(2,1)} %bitcast_select_fusion), calls=%async_computation.2 | async-start | bytes 32768 | tf_op jit(solution)/shard_map/all_to_all | solution.py:74
Sparse Core Ops, SparseCore 0:
  390.9 621.1 reduce-scatter.1
where the time goes:
time: 1060 us
  waiting for transfers between devices  579 us (55%)
  local copies, waits for them, and re-layouts  177 us (17%)
  blocking collectives  129 us (12%)
  other arithmetic  122 us (12%)
  matrix products  23.7 us (2%)
  between operations  14.3 us (1%)
    reduce_scatter x1, waiting for transfers between devices, on_device(): lax.psum_scatter(gram_panel.reshape(params, per_owner * tile_width).astyp...  579 us
    all_gather x1, blocking collectives, on_device(): lax.all_gather(owner_of, 'tile', axis=0, tiled=True)  97 us
    unnamed x22, local copies, waits for them, and re-layouts  65.6 us
    scatter-add x1, other arithmetic, on_device(): gram_panel = gram_panel.at[col_flat, :, sub_flat[:, None], :].add(item_prod)  52.8 us
    convert_element_type x1, local copies, waits for them, and re-layouts, on_device(): gram_panel.reshape(params, per_owner * tile_width).astype(jnp.bfloat16)  46.2 us
    convert_element_type x1, other arithmetic, on_device(): gram_panel.reshape(params, per_owner * tile_width).astype(jnp.bfloat16)  36.4 us
    broadcast_in_dim x1, local copies, waits for them, and re-layouts, on_device(): jnp.zeros((tile_count, tile_width, per_owner, tile_width), jnp.float32)  23.9 us
  transfers between devices with their start and end apart: 3, of which 1 were waited for; matrix products, arithmetic and copies ran while one was open for 3% of the time, Pallas kernels for 0%

commit v1 on v0

v1 whole, which is shorter than its diff:
```python
import functools

import jax
import jax.numpy as jnp
from jax import lax
from jax.experimental import pallas as pl
from jax.experimental.pallas import tpu as pltpu
from jax.sharding import PartitionSpec as P

huber_limit = 1.345


def weigh_kernel(tile_ids, sigma, estimate, design, observed, obs_type, weighted, pull):
    blocks, _, row_width = design.shape
    tile_width = row_width // 4
    for block in range(blocks):
        rows = design[block].astype(jnp.float32)
        touched = jnp.concatenate(
            [estimate[pl.ds(tile_ids[4 * block + part], 1), :] for part in range(4)], axis=1
        )
        predicted = jnp.sum(rows * touched, axis=1, keepdims=True)
        residual = observed[:, block : block + 1] - predicted
        types = obs_type[:, block : block + 1]
        spread = jnp.zeros_like(residual)
        for code in range(sigma.shape[0]):
            spread = jnp.where(types == code, sigma[code], spread)
        scaled = jnp.abs(residual) / spread
        root_weight = jnp.sqrt(huber_limit / jnp.maximum(scaled, huber_limit)) / spread
        scaled_rows = (root_weight * rows).astype(jnp.bfloat16)
        target = (root_weight * residual).astype(jnp.bfloat16).astype(jnp.float32)
        weighted[block] = scaled_rows
        pull[block : block + 1, :] = jnp.sum(
            scaled_rows.astype(jnp.float32) * target, axis=0, keepdims=True
        )


def weigh(tile_ids, sigma, estimate, design, observed, obs_type):
    blocks, block_rows, row_width = design.shape
    smem, vmem = pl.BlockSpec(memory_space=pltpu.SMEM), pl.BlockSpec(memory_space=pltpu.VMEM)
    return pl.pallas_call(
        weigh_kernel,
        out_shape=(
            jax.ShapeDtypeStruct(design.shape, jnp.bfloat16),
            jax.ShapeDtypeStruct((blocks, row_width), jnp.float32),
        ),
        in_specs=[smem, smem, vmem, vmem, vmem, vmem],
        out_specs=(vmem, vmem),
        compiler_params=pltpu.CompilerParams(vmem_limit_bytes=16 << 20),
        name="weigh",
    )(tile_ids, sigma, estimate, design, observed.T, obs_type.T)


def gram_kernel(row_groups, table, items, pull, prior, normal, gradient, total, grad_total, sem):
    step = pl.program_id(0)
    chunk, _, row_width = items.shape
    tile_width = row_width // 4
    kept = normal.shape[0]
    load = pltpu.make_async_copy(prior, total.at[pl.ds(0, kept)], sem)

    @pl.when(step == 0)
    def _():
        load.start()
        grad_total[...] = jnp.zeros_like(grad_total)
        load.wait()

    fields = 2 + 2 * row_groups
    for item in range(chunk):
        base = (step * chunk + item) * fields

        def lanes(entry):
            return pl.ds(pl.multiple_of(table[base + entry] * tile_width, tile_width), tile_width)

        part = lanes(0)
        sub = table[base + 1]
        column = pl.ds(
            pl.multiple_of(jnp.minimum(sub, gradient.shape[0] - 1) * tile_width, tile_width),
            tile_width,
        )
        grad_total[pl.ds(sub, 1), :] += pull[pl.ds(item, 1), part]
        left = jnp.concatenate(
            [items[item, :, lanes(2 + 2 * group)] for group in range(row_groups)], axis=1
        )
        products = lax.dot_general(
            left,
            items[item, :, part],
            (((0,), (0,)), ((), ())),
            preferred_element_type=jnp.float32,
        )
        for group in range(row_groups):
            total[lanes(3 + 2 * group), column] += products[
                group * tile_width : (group + 1) * tile_width
            ]

    @pl.when(step == pl.num_programs(0) - 1)
    def _():
        store = pltpu.make_async_copy(total.at[pl.ds(0, kept)], normal, sem)
        store.start()
        gradient[...] = grad_total[: gradient.shape[0]]
        store.wait()


def gram(table, items, pull, prior, per_owner, row_groups, chunk):
    count, block_rows, row_width = items.shape
    tile_width = row_width // 4
    kept, width = prior.shape
    padded = -(-(per_owner + 1) // 8) * 8
    return pl.pallas_call(
        functools.partial(gram_kernel, row_groups),
        grid_spec=pltpu.PrefetchScalarGridSpec(
            num_scalar_prefetch=1,
            grid=(count // chunk,),
            in_specs=[
                pl.BlockSpec((chunk, block_rows, row_width), lambda step, table: (step, 0, 0)),
                pl.BlockSpec((chunk, row_width), lambda step, table: (step, 0)),
                pl.BlockSpec(memory_space=pl.ANY),
            ],
            out_specs=(
                pl.BlockSpec(memory_space=pl.ANY),
                pl.BlockSpec((per_owner, tile_width), lambda step, table: (0, 0)),
            ),
            scratch_shapes=[
                pltpu.VMEM((kept + tile_width, width), jnp.float32),
                pltpu.VMEM((padded, tile_width), jnp.float32),
                pltpu.SemaphoreType.DMA,
            ],
        ),
        out_shape=(
            jax.ShapeDtypeStruct(prior.shape, jnp.float32),
            jax.ShapeDtypeStruct((per_owner, tile_width), jnp.float32),
        ),
        compiler_params=pltpu.CompilerParams(
            vmem_limit_bytes=(kept + tile_width) * width * 4 + (12 << 20)
        ),
        name="gram",
    )(table, items, pull, prior)

MESH = pl.DeviceIdType.MESH
routes = ("zxy", "zyx", "xzy", "yzx")


def spread_kernel(n_arc, shard, small, whole, whole_small, *sems):
    far_send, far_recv, small_send, small_recv, own_sem = sems
    arc, tile = lax.axis_index("arc"), lax.axis_index("tile")
    y, x, core = tile // 4, (tile // 2) % 2, tile % 2

    def at(y, x, core):
        return y * 4 + x * 2 + core

    links = {
        "x": (0, (arc, at(y, 1 - x, core)), None),
        "y": (1, (arc, at(1 - y, x, core)), None),
        "up": (2, (arc + 1, tile), arc + 1 < n_arc),
        "down": (3, (arc - 1, tile), arc > 0),
        "core": (4, (arc, at(y, x, 1 - core)), None),
    }

    def when(*conditions):
        conditions = [condition for condition in conditions if condition is not None]
        if not conditions:
            return lambda body: body()
        return pl.when(functools.reduce(jnp.logical_and, conditions))

    barrier = pltpu.get_barrier_semaphore()
    for _, device, there in links.values():

        @when(there)
        def _(device=device):
            pl.semaphore_signal(barrier, inc=1, device_id=device, device_id_type=MESH)

    pl.semaphore_wait(
        barrier, 3 + (arc + 1 < n_arc).astype(jnp.int32) + (arc > 0).astype(jnp.int32)
    )

    me = arc * 8 + tile
    keep = [
        pltpu.make_async_copy(shard, whole.at[me], own_sem.at[0]),
        pltpu.make_async_copy(small, whole_small.at[me], own_sem.at[1]),
    ]
    for copy in keep:
        copy.start()

    share = shard.shape[0] // len(routes)

    def copies(route, far, link, own=False, other=False):
        far_x, far_y, far_z = far
        from_y = 1 - y if far_y else y
        from_x = 1 - x if far_x else x
        chip = (arc + far_z) * 4 + from_y * 2 + from_x
        source = (arc + far_z) * 8 + at(from_y, from_x, 1 - core if other else core)
        number, device, _ = links[link]
        rows = pl.ds(route * share, share)
        arrive = 1 if other or link == "core" else 0
        made = [
            pltpu.make_async_remote_copy(
                src_ref=shard.at[rows] if own else whole.at[source, rows],
                dst_ref=whole.at[source, rows],
                send_sem=far_send.at[route, chip, number],
                recv_sem=far_recv.at[route, chip, arrive],
                device_id=device,
                device_id_type=MESH,
            )
        ]
        if route == 0:
            made.append(
                pltpu.make_async_remote_copy(
                    src_ref=small if own else whole_small.at[source],
                    dst_ref=whole_small.at[source],
                    send_sem=small_send.at[chip, number],
                    recv_sem=small_recv.at[chip, arrive],
                    device_id=device,
                    device_id_type=MESH,
                )
            )
        return made

    def onward(route, far):
        offsets = dict(zip("xyz", far))
        order = routes[route]
        last = max([order.index(axis) for axis in "xyz" if offsets[axis]], default=-1)
        out = []
        if last >= 0 and order[last] == "z":
            out.append("up" if far[2] < 0 else "down")
        for axis in order[last + 1 :]:
            out += ["up", "down"] if axis == "z" else [axis]
        return out + ["core"]

    offsets = [(i, j, k) for i in range(2) for j in range(2) for k in range(1 - n_arc, n_arc)]
    offsets.sort(key=lambda far: (far[0] + far[1] + abs(far[2]), far))
    sent = []
    for far in offsets:
        held = None if far[2] == 0 else (arc + far[2] >= 0 if far[2] < 0 else arc + far[2] < n_arc)

        @when(held)
        def _(far=far, own=far == (0, 0, 0)):
            for route in range(len(routes)):
                if not own:
                    for copy in copies(route, far, "x"):
                        copy.wait_recv()
                for link in onward(route, far):

                    @when(links[link][2])
                    def _(route=route, link=link):
                        for copy in copies(route, far, link, own):
                            copy.start()

    for far in offsets:
        held = None if far[2] == 0 else (arc + far[2] >= 0 if far[2] < 0 else arc + far[2] < n_arc)

        @when(held)
        def _(far=far, own=far == (0, 0, 0)):
            for route in range(len(routes)):
                for copy in copies(route, far, "core", other=True):
                    copy.wait_recv()
                for link in onward(route, far):

                    @when(links[link][2])
                    def _(route=route, link=link):
                        for copy in copies(route, far, link, own):
                            copy.wait_send()

    for copy in keep:
        copy.wait()


def spread_out(shard, small, n_arc):
    devices = n_arc * 8
    hbm = pl.BlockSpec(memory_space=pl.ANY)
    dma = pltpu.SemaphoreType.DMA
    whole, whole_small = pl.pallas_call(
        functools.partial(spread_kernel, n_arc),
        out_shape=(
            jax.ShapeDtypeStruct((devices, *shard.shape), shard.dtype),
            jax.ShapeDtypeStruct((devices, *small.shape), small.dtype),
        ),
        in_specs=[hbm, hbm],
        out_specs=(hbm, hbm),
        scratch_shapes=[
            dma((len(routes), n_arc * 4, 5)),
            dma((len(routes), n_arc * 4, 2)),
            dma((n_arc * 4, 5)),
            dma((n_arc * 4, 2)),
            dma((2,)),
        ],
        compiler_params=pltpu.CompilerParams(collective_id=0, has_side_effects=True),
        name="spread",
    )(shard, small)
    return whole.reshape(-1, *shard.shape[1:]), whole_small.reshape(-1, small.shape[1])


def item_table(ids, arc, owner, per_owner, row_groups):
    slots = jnp.arange(4, dtype=jnp.int32)
    owners = jnp.where(ids < 0, -1, ids // per_owner)

    def find(wanted):
        hit = owners == wanted
        return jnp.any(hit, axis=1), jnp.sum(jnp.where(hit, slots, 0), axis=1), jnp.sum(
            jnp.where(hit, ids - wanted * per_owner, 0), axis=1
        )

    named, slot, sub = find(owner)
    fields = [slot, jnp.where(named, sub, per_owner)]
    for group in range(row_groups):
        found, row_slot, row_sub = find(arc * row_groups + group)
        fields += [
            row_slot,
            jnp.where(named & found, group * per_owner + row_sub, row_groups * per_owner),
        ]
    return jnp.stack(fields, axis=1).reshape(-1)


def pack_slots(owner_of, n_owner, capacity):
    named = jnp.any(
        owner_of[None] == jnp.arange(n_owner, dtype=jnp.int32)[:, None, None], axis=2
    )
    rank = jnp.cumsum(named.astype(jnp.int32), axis=1) - 1
    chosen = named[:, None, :] & (
        rank[:, None, :] == jnp.arange(capacity, dtype=jnp.int32)[None, :, None]
    )
    block_ids = jnp.arange(owner_of.shape[0], dtype=jnp.int32)
    return jnp.any(chosen, axis=2), jnp.sum(jnp.where(chosen, block_ids, 0), axis=2)


def on_device(design, observed, obs_type, owner_of, sub_of, sigma_table, solution, prior):
    n_arc, n_owner = lax.axis_size("arc"), lax.axis_size("tile")
    blocks, block_rows, row_width = design.shape
    tile_width = row_width // 4
    per_owner = solution.shape[0] // tile_width
    row_groups = n_owner // n_arc
    capacity = 2 * ((4 * blocks + n_owner - 1) // n_owner)
    everyone = ("arc", "tile")
    tile_ids = owner_of * per_owner + sub_of
    by_route = n_owner == 8 and capacity >= blocks and blocks % len(routes) == 0
    if by_route:
        mine = jnp.zeros((-(-(solution.shape[0] + 4 * blocks) // 1024) * 1024,), jnp.float32)
        mine = mine.at[: solution.shape[0]].set(solution)
        mine = mine.at[solution.shape[0] : solution.shape[0] + 4 * blocks].set(
            tile_ids.reshape(-1).astype(jnp.float32)
        )
        both = lax.all_gather(mine.reshape(-1, tile_width), everyone, axis=0, tiled=True)
        both = both.reshape(n_arc * n_owner, -1, tile_width)
        whole_solution = both[:n_owner, :per_owner]
        all_ids = both[:, per_owner:].reshape(n_arc * n_owner, -1)[:, : 4 * blocks]
        all_ids = all_ids.astype(jnp.int32).reshape(-1, 4)
    else:
        whole_solution = lax.all_gather(solution, "tile", axis=0, tiled=True)
    weighted, pull = weigh(
        tile_ids.reshape(-1),
        sigma_table,
        whole_solution.reshape(-1, tile_width),
        design,
        observed,
        obs_type,
    )
    if by_route:
        items, pull = spread_out(weighted, pull, n_arc)
        tile_ids = all_ids
    else:
        gathered = everyone
        if capacity < blocks:
            live, block = pack_slots(owner_of, n_owner, capacity)
            over_tile = functools.partial(
                lax.all_to_all, axis_name="tile", split_axis=0, concat_axis=0, tiled=True
            )
            weighted = over_tile(weighted[block].reshape(-1, block_rows, row_width))
            pull = over_tile(pull[block].reshape(-1, row_width))
            tile_ids = over_tile(jnp.where(live[:, :, None], tile_ids[block], -1).reshape(-1, 4))
            gathered = "arc"
        tile_ids = lax.all_gather(tile_ids, gathered, axis=0, tiled=True)
        pull = lax.all_gather(pull, gathered, axis=0, tiled=True)
        items = lax.all_gather(weighted, gathered, axis=0, tiled=True)
    table = item_table(
        tile_ids, lax.axis_index("arc"), lax.axis_index("tile"), per_owner, row_groups
    )
    normal, gradient = gram(table, items, pull, prior, per_owner, row_groups, blocks)
    return normal, gradient.reshape(-1)


def solution(mesh):
    in_specs = (
        P(("arc", "tile"), None, None),
        P(("arc", "tile"), None),
        P(("arc", "tile"), None),
        P(("arc", "tile"), None),
        P(("arc", "tile"), None),
        P(),
        P("tile"),
        P("arc", "tile"),
    )
    out_specs = (P("arc", "tile"), P("tile"))
    return jax.shard_map(
        on_device, mesh=mesh, in_specs=in_specs, out_specs=out_specs, check_vma=False
    )
```

time: 1060 us -> 231 us (0.22)
  waiting for transfers between devices: 579 us -> 0 us
  Pallas kernels: 0 us -> 170 us
  local copies, waits for them, and re-layouts: 177 us -> 14.2 us
  other arithmetic: 122 us -> 1.35 us
  blocking collectives: 129 us -> 43.9 us
  matrix products: 23.7 us -> 0 us
  between operations: 14.3 us -> 0.8 us
    reduce_scatter x1 -> x0, waiting for transfers between devices: 579 us -> none  [on_device(): lax.psum_scatter(gram_panel.reshape(params, per_owner * tile_width).astyp...]
    pallas_call x0 -> x3, Pallas kernels: none -> 170 us  [the longest x1 131 us: spread_out(): pl.pallas_call(functools.partial(spread_kernel, n_arc), out_shape=(jax.Sh...]
    all_gather x3 -> x1, blocking collectives: 116 us -> 43.9 us  [on_device(): lax.all_gather(mine.reshape(-1, tile_width), everyone, axis=0, tiled=True)]
    scatter-add x2 -> x0, other arithmetic: 53.7 us -> none  [the longest x1 52.8 us: on_device(): gram_panel = gram_panel.at[col_flat, :, sub_flat[:, None], :].add(item_prod)]
    unnamed x22 -> x15, local copies, waits for them, and re-layouts: 65.6 us -> 12.4 us
    convert_element_type x1 -> x0, local copies, waits for them, and re-layouts: 46.2 us -> none  [on_device(): gram_panel.reshape(params, per_owner * tile_width).astype(jnp.bfloat16)]
    convert_element_type x3 -> x0, other arithmetic: 39.2 us -> none  [the longest x1 36.4 us: on_device(): gram_panel.reshape(params, per_owner * tile_width).astype(jnp.bfloat16)]
    gather x14 -> x0, local copies, waits for them, and re-layouts: 25.7 us -> none  [the longest x2 16.9 us: on_device(): weighted.reshape(blocks, block_rows, row_width)[send_block]]
  transfers between devices with their start and end apart: 3 -> 0, of which waited for: 1 -> 0; matrix products, arithmetic and copies ran while one was open for 3% -> 0% of each run, Pallas kernels for 0% -> 0%
where the time goes in v1:
time: 231 us; the launch traced here: 230 us
  Pallas kernels  170 us (74%)
  blocking collectives  43.9 us (19%)
  local copies, waits for them, and re-layouts  14.2 us (6%)
    pallas_call x1, Pallas kernels, spread_out(): pl.pallas_call(functools.partial(spread_kernel, n_arc), out_shape=(jax.Sh...  131 us
    all_gather x1, blocking collectives, on_device(): lax.all_gather(mine.reshape(-1, tile_width), everyone, axis=0, tiled=True)  43.9 us
    pallas_call x1, Pallas kernels, gram(): pl.pallas_call(functools.partial(gram_kernel, row_groups), grid_spec=pltp...  37.1 us
    unnamed x15, local copies, waits for them, and re-layouts  12.4 us

profile of v1, /device:TPU:0, one launch (start us, length us, event | category | flops | bytes accessed | tf_op | source)
XLA Modules:
  0.0 230.2 jit_solution(14294741890690043477)
XLA Ops:
  0.6 0.7 multiply_add_fusion
  1.5 0.7 scatter.6
  2.2 0.8 copy.15
  3.0 0.8 copy.16
  3.8 43.9 %all_gather.3 = f32[512,128]{1,0:T(8,128)S(1)} all-gather(f32[16,128]{1,0:T(8,128)S(1)} %bitcast.26), channel_id=1, replica_groups=mesh['arc'=4,'tile'=8] {'arc','tile'}, dimensions={0}, use_global_device_ids=true | all-gather | bytes 270336 | tf_op jit(solution)/shard_map/all_gather | solution.py:339
  47.8 0.1 and.38
  47.9 0.1 lt.13
  48.1 0.1 sub.42
  48.3 0.2 fusion.7
  48.5 0.1 sub.36
  48.6 0.2 select_reduce_fusion.4
  48.7 0.1 sub.39
  48.8 0.2 select_reduce_fusion
  49.1 0.1 copy.14
  49.3 0.1 reshape.156.table
  49.4 1.2 copy-done.1
  50.6 0.7 copy-done.5
  51.3 1.9 weigh.1
  53.2 1.0 copy-done.2
  54.1 0.6 copy-done.4
  54.7 131.0 %spread.1 = (bf16[32,8,128,512]{3,2,1,0:T(8,128)(2,1)}, f32[32,8,512]{2,1,0:T(8,128)}) custom-call(bf16[8,128,512]{2,1,0:T(8,128)(2,1)} %copy-done.2, f32[8,512]{1,0:T(8,128)} %copy-done.4), custom_call_target="tpu_custom_call" | custom-call | tf_op jit(solution)/shard_map/spread/pallas_call | solution.py:269
  185.8 6.4 %copy-done = f32[3072,1536]{1,0:T(8,128)S(1)} copy-done((f32[3072,1536]{1,0:T(8,128)S(1)}, f32[3072,1536]{1,0:T(8,128)}, u32[]{:S(2)}) %copy-start) | copy-done | bytes 18874392
  192.1 1.0 copy-done.3
  193.2 37.1 %gram.1 = (f32[3072,1536]{1,0:T(8,128)}, f32[12,128]{1,0:T(8,128)}) custom-call(s32[1536]{0:T(1024)S(1)} %reshape.156.table, bf16[256,128,512]{2,1,0:T(8,128)(2,1)} %bitcast.20, f32[256,512]{1,0:T(8,128)S(1)} %bitcast.17, f32[3072,1536]{1,0:T(8,128)S(1)} %copy-done), custom_call_target="tpu_custom_call" | custom-call | tf_op jit(solution)/shard_map/gram/pallas_call | solution.py:107
  (18 shorter events, 0.4 us)
Async XLA Ops:
  49.4 1.2 copy-start.1
  50.6 0.7 copy-start.5
  53.1 1.0 copy-start.2
  54.1 0.6 copy-start.4
  185.7 6.4 %copy-start = (f32[3072,1536]{1,0:T(8,128)S(1)}, f32[3072,1536]{1,0:T(8,128)}, u32[]{:S(2)}) copy-start(f32[3072,1536]{1,0:T(8,128)} %prior.1) | copy-start | bytes 56623108
  192.1 1.0 copy-start.3

commit v2 on v1

--- a/solution.py
+++ b/solution.py
@@ -10,27 +10,32 @@
 huber_limit = 1.345
 
 
+def weigh_block(rows, touched, observed, types, sigma):
+    rows = rows.astype(jnp.float32)
+    residual = observed - jnp.sum(rows * touched, axis=1, keepdims=True)
+    spread = jnp.zeros_like(residual)
+    for code in range(sigma.shape[0]):
+        spread = jnp.where(types == code, sigma[code], spread)
+    scaled = jnp.abs(residual) / spread
+    root_weight = jnp.sqrt(huber_limit / jnp.maximum(scaled, huber_limit)) / spread
+    scaled_rows = (root_weight * rows).astype(jnp.bfloat16)
+    target = (root_weight * residual).astype(jnp.bfloat16).astype(jnp.float32)
+    return scaled_rows, jnp.sum(
+        scaled_rows.astype(jnp.float32) * target, axis=0, keepdims=True
+    )
+
+
 def weigh_kernel(tile_ids, sigma, estimate, design, observed, obs_type, weighted, pull):
-    blocks, _, row_width = design.shape
-    tile_width = row_width // 4
-    for block in range(blocks):
-        rows = design[block].astype(jnp.float32)
+    for block in range(design.shape[0]):
         touched = jnp.concatenate(
             [estimate[pl.ds(tile_ids[4 * block + part], 1), :] for part in range(4)], axis=1
         )
-        predicted = jnp.sum(rows * touched, axis=1, keepdims=True)
-        residual = observed[:, block : block + 1] - predicted
-        types = obs_type[:, block : block + 1]
-        spread = jnp.zeros_like(residual)
-        for code in range(sigma.shape[0]):
-            spread = jnp.where(types == code, sigma[code], spread)
-        scaled = jnp.abs(residual) / spread
-        root_weight = jnp.sqrt(huber_limit / jnp.maximum(scaled, huber_limit)) / spread
-        scaled_rows = (root_weight * rows).astype(jnp.bfloat16)
-        target = (root_weight * residual).astype(jnp.bfloat16).astype(jnp.float32)
-        weighted[block] = scaled_rows
-        pull[block : block + 1, :] = jnp.sum(
-            scaled_rows.astype(jnp.float32) * target, axis=0, keepdims=True
+        weighted[block], pull[block : block + 1, :] = weigh_block(
+            design[block],
+            touched,
+            observed[:, block : block + 1],
+            obs_type[:, block : block + 1],
+            sigma,
         )
 
 
@@ -111,7 +116,7 @@
             grid=(count // chunk,),
             in_specs=[
                 pl.BlockSpec((chunk, block_rows, row_width), lambda step, table: (step, 0, 0)),
-                pl.BlockSpec((chunk, row_width), lambda step, table: (step, 0)),
+                pl.BlockSpec((chunk, pull.shape[1]), lambda step, table: (step, 0)),
                 pl.BlockSpec(memory_space=pl.ANY),
             ],
             out_specs=(
@@ -129,7 +134,7 @@
             jax.ShapeDtypeStruct((per_owner, tile_width), jnp.float32),
         ),
         compiler_params=pltpu.CompilerParams(
-            vmem_limit_bytes=(kept + tile_width) * width * 4 + (12 << 20)
+            vmem_limit_bytes=56 << 20
         ),
         name="gram",
     )(table, items, pull, prior)
@@ -138,8 +143,24 @@
 routes = ("zxy", "zyx", "xzy", "yzx")
 
 
-def spread_kernel(n_arc, shard, small, whole, whole_small, *sems):
-    far_send, far_recv, small_send, small_recv, own_sem = sems
+def spread_kernel(
+    n_arc,
+    owner_of,
+    sub_of,
+    sigma,
+    solution,
+    numbers,
+    design,
+    observed,
+    obs_type,
+    whole,
+    whole_small,
+    estimate,
+    shard,
+    small,
+    *sems,
+):
+    far_send, far_recv, small_send, small_recv, own_sem, early_send, early_recv = sems
     arc, tile = lax.axis_index("arc"), lax.axis_index("tile")
     y, x, core = tile // 4, (tile // 2) % 2, tile % 2
 
@@ -172,12 +193,43 @@
     )
 
     me = arc * 8 + tile
-    keep = [
-        pltpu.make_async_copy(shard, whole.at[me], own_sem.at[0]),
-        pltpu.make_async_copy(small, whole_small.at[me], own_sem.at[1]),
-    ]
-    for copy in keep:
+    first = pltpu.make_async_copy(solution, estimate.at[tile], own_sem.at[0])
+    first.start()
+    first.wait()
+    for stage, (link, start, length) in enumerate(
+        [("core", tile, 1), ("x", tile // 2 * 2, 2), ("y", tile // 4 * 4, 4)]
+    ):
+        held = estimate.at[pl.ds(start, length)]
+        copy = pltpu.make_async_remote_copy(
+            src_ref=held,
+            dst_ref=held,
+            send_sem=early_send.at[stage],
+            recv_sem=early_recv.at[stage],
+            device_id=links[link][1],
+            device_id_type=MESH,
+        )
         copy.start()
+        copy.wait()
+
+    row_width = design.shape[2]
+    small[:, row_width:] = numbers[...]
+
+    def weigh_share(route):
+        for block in range(route * share, (route + 1) * share):
+            touched = jnp.concatenate(
+                [
+                    estimate[owner_of[4 * block + part], pl.ds(sub_of[4 * block + part], 1), :]
+                    for part in range(4)
+                ],
+                axis=1,
+            )
+            shard[block], small[block : block + 1, :row_width] = weigh_block(
+                design[block],
+                touched,
+                observed[:, block : block + 1],
+                obs_type[:, block : block + 1],
+                sigma,
+            )
 
     share = shard.shape[0] // len(routes)
 
@@ -200,7 +252,7 @@
                 device_id_type=MESH,
             )
         ]
-        if route == 0:
+        if route == len(routes) - 1:
             made.append(
                 pltpu.make_async_remote_copy(
                     src_ref=small if own else whole_small.at[source],
@@ -226,14 +278,15 @@
 
     offsets = [(i, j, k) for i in range(2) for j in range(2) for k in range(1 - n_arc, n_arc)]
     offsets.sort(key=lambda far: (far[0] + far[1] + abs(far[2]), far))
-    sent = []
     for far in offsets:
         held = None if far[2] == 0 else (arc + far[2] >= 0 if far[2] < 0 else arc + far[2] < n_arc)
 
         @when(held)
         def _(far=far, own=far == (0, 0, 0)):
             for route in range(len(routes)):
-                if not own:
+                if own:
+                    weigh_share(route)
+                else:
                     for copy in copies(route, far, "x"):
                         copy.wait_recv()
                 for link in onward(route, far):
@@ -242,6 +295,14 @@
                     def _(route=route, link=link):
                         for copy in copies(route, far, link, own):
                             copy.start()
+
+        if far == (0, 0, 0):
+            keep = [
+                pltpu.make_async_copy(shard, whole.at[me], own_sem.at[0]),
+                pltpu.make_async_copy(small, whole_small.at[me], own_sem.at[1]),
+            ]
+            for copy in keep:
+                copy.start()
 
     for far in offsets:
         held = None if far[2] == 0 else (arc + far[2] >= 0 if far[2] < 0 else arc + far[2] < n_arc)
@@ -262,29 +323,48 @@
         copy.wait()
 
 
-def spread_out(shard, small, n_arc):
+def spread_out(owner_of, sub_of, sigma, solution, numbers, design, observed, obs_type, n_arc):
     devices = n_arc * 8
-    hbm = pl.BlockSpec(memory_space=pl.ANY)
+    blocks, block_rows, row_width = design.shape
+    hbm, vmem = pl.BlockSpec(memory_space=pl.ANY), pl.BlockSpec(memory_space=pltpu.VMEM)
+    smem = pl.BlockSpec(memory_space=pltpu.SMEM)
     dma = pltpu.SemaphoreType.DMA
+    small = (blocks, row_width + numbers.shape[1])
     whole, whole_small = pl.pallas_call(
         functools.partial(spread_kernel, n_arc),
         out_shape=(
-            jax.ShapeDtypeStruct((devices, *shard.shape), shard.dtype),
-            jax.ShapeDtypeStruct((devices, *small.shape), small.dtype),
-        ),
-        in_specs=[hbm, hbm],
+            jax.ShapeDtypeStruct((devices, *design.shape), jnp.bfloat16),
+            jax.ShapeDtypeStruct((devices, *small), jnp.float32),
+        ),
+        in_specs=[smem, smem, smem, vmem, vmem, vmem, vmem, vmem],
         out_specs=(hbm, hbm),
         scratch_shapes=[
+            pltpu.VMEM((8, *solution.shape), jnp.float32),
+            pltpu.VMEM(design.shape, jnp.bfloat16),
+            pltpu.VMEM(small, jnp.float32),
             dma((len(routes), n_arc * 4, 5)),
             dma((len(routes), n_arc * 4, 2)),
             dma((n_arc * 4, 5)),
             dma((n_arc * 4, 2)),
             dma((2,)),
+            dma((3,)),
+            dma((3,)),
         ],
-        compiler_params=pltpu.CompilerParams(collective_id=0, has_side_effects=True),
+        compiler_params=pltpu.CompilerParams(
+            collective_id=0, has_side_effects=True, vmem_limit_bytes=56 << 20
+        ),
         name="spread",
-    )(shard, small)
-    return whole.reshape(-1, *shard.shape[1:]), whole_small.reshape(-1, small.shape[1])
+    )(
+        owner_of.reshape(-1),
+        sub_of.reshape(-1),
+        sigma,
+        solution,
+        numbers,
+        design,
+        observed.T,
+        obs_type.T,
+    )
+    return whole.reshape(-1, block_rows, row_width), whole_small.reshape(-1, small[1])
 
 
 def item_table(ids, arc, owner, per_owner, row_groups):
@@ -331,30 +411,29 @@
     tile_ids = owner_of * per_owner + sub_of
     by_route = n_owner == 8 and capacity >= blocks and blocks % len(routes) == 0
     if by_route:
-        mine = jnp.zeros((-(-(solution.shape[0] + 4 * blocks) // 1024) * 1024,), jnp.float32)
-        mine = mine.at[: solution.shape[0]].set(solution)
-        mine = mine.at[solution.shape[0] : solution.shape[0] + 4 * blocks].set(
-            tile_ids.reshape(-1).astype(jnp.float32)
-        )
-        both = lax.all_gather(mine.reshape(-1, tile_width), everyone, axis=0, tiled=True)
-        both = both.reshape(n_arc * n_owner, -1, tile_width)
-        whole_solution = both[:n_owner, :per_owner]
-        all_ids = both[:, per_owner:].reshape(n_arc * n_owner, -1)[:, : 4 * blocks]
-        all_ids = all_ids.astype(jnp.int32).reshape(-1, 4)
+        numbers = jnp.pad(tile_ids.astype(jnp.float32), ((0, 0), (0, tile_width - 4)))
+        items, pull = spread_out(
+            owner_of,
+            sub_of,
+            sigma_table,
+            solution.reshape(per_owner, tile_width),
+            numbers,
+            design,
+            observed,
+            obs_type,
+            n_arc,
+        )
+        tile_ids = pull[:, row_width : row_width + 4].astype(jnp.int32)
     else:
         whole_solution = lax.all_gather(solution, "tile", axis=0, tiled=True)
-    weighted, pull = weigh(
-        tile_ids.reshape(-1),
-        sigma_table,
-        whole_solution.reshape(-1, tile_width),
-        design,
-        observed,
-        obs_type,
-    )
-    if by_route:
-        items, pull = spread_out(weighted, pull, n_arc)
-        tile_ids = all_ids
-    else:
+        weighted, pull = weigh(
+            tile_ids.reshape(-1),
+            sigma_table,
+            whole_solution.reshape(-1, tile_width),
+            design,
+            observed,
+            obs_type,
+        )
         gathered = everyone
         if capacity < blocks:
             live, block = pack_slots(owner_of, n_owner, capacity)

time: 231 us -> 194 us (0.84)
  blocking collectives: 43.9 us -> 0 us
  Pallas kernels: 170 us -> 183 us
  local copies, waits for them, and re-layouts: 14.2 us -> 7.02 us
    all_gather x1 -> x0, blocking collectives: 43.9 us -> none  [on_device(): lax.all_gather(mine.reshape(-1, tile_width), everyone, axis=0, tiled=True)]
    pallas_call x1, Pallas kernels: 131 us -> 140 us  [spread_out(): pl.pallas_call(functools.partial(spread_kernel, n_arc), out_shape=(jax.Sh...]
    unnamed x15 -> x4, local copies, waits for them, and re-layouts: 12.4 us -> 4.33 us
    pallas_call x1, Pallas kernels: 37.1 us -> 42.4 us  [gram(): pl.pallas_call(functools.partial(gram_kernel, row_groups), grid_spec=pltp...]
where the time goes in v2:
time: 194 us; the launch traced here: 193 us
  Pallas kernels  183 us (94%)
  local copies, waits for them, and re-layouts  7.02 us (4%)
  other arithmetic  2.47 us (1%)
    pallas_call x1, Pallas kernels, spread_out(): pl.pallas_call(functools.partial(spread_kernel, n_arc), out_shape=(jax.Sh...  140 us
    pallas_call x1, Pallas kernels, gram(): pl.pallas_call(functools.partial(gram_kernel, row_groups), grid_spec=pltp...  42.4 us
    unnamed x4, local copies, waits for them, and re-layouts  4.33 us

profile of v2, /device:TPU:0, one launch (start us, length us, event | category | flops | bytes accessed | tf_op | source)
XLA Modules:
  0.0 192.8 jit_solution(814895932502669676)
XLA Ops:
  0.6 0.8 copy.16
  1.4 0.6 reshape.85.owner_of
  2.0 0.8 copy.17
  2.8 0.6 reshape.86.sub_of
  3.4 0.6 pad.4.numbers
  4.0 1.4 copy.20
  5.4 1.4 copy.21
  6.8 140.2 %spread.1 = (bf16[32,8,128,512]{3,2,1,0:T(8,128)(2,1)}, f32[32,8,640]{2,1,0:T(8,128)}) custom-call(s32[32]{0:T(128)} %reshape.85.owner_of, s32[32]{0:T(128)} %reshape.86.sub_of, f32[8]{0:T(128)} %sigma.1, f32[12,128]{1,0:T(8,128)} %bitcast.18, f32[8,128]{1,0:T(8,128)} %pad.4.numbers, bf16[8,128,512]{2,1,0:T(8,128)(2,1)} %design.1, f32[128,8]{1,0:T(8,128)} %bitcast.16, ...), custom_call_target="tpu_custom_call" | custom-call | tf_op jit(solution)/shard_map/spread/pallas_call | solution.py:333
  147.0 1.1 fusion.2
  148.1 0.1 fusion.5
  148.3 1.2 select_reduce_fusion
  149.5 0.1 copy.22
  149.6 0.7 reshape.89.table
  150.4 42.4 %gram.1 = (f32[3072,1536]{1,0:T(8,128)}, f32[12,128]{1,0:T(8,128)}) custom-call(s32[1536]{0:T(1024)} %reshape.89.table, bf16[256,128,512]{2,1,0:T(8,128)(2,1)} %bitcast.12, f32[256,640]{1,0:T(8,128)} %bitcast.15, f32[3072,1536]{1,0:T(8,128)} %prior.1), custom_call_target="tpu_custom_call" | custom-call | tf_op jit(solution)/shard_map/gram/pallas_call | solution.py:112
  (3 shorter events, 0.0 us)

commit v3 on v2

--- a/solution.py
+++ b/solution.py
@@ -141,6 +141,7 @@
 
 MESH = pl.DeviceIdType.MESH
 routes = ("zxy", "zyx", "xzy", "yzx")
+shares = (3, 3, 5, 5)
 
 
 def spread_kernel(
@@ -149,7 +150,6 @@
     sub_of,
     sigma,
     solution,
-    numbers,
     design,
     observed,
     obs_type,
@@ -211,27 +211,34 @@
         copy.start()
         copy.wait()
 
-    row_width = design.shape[2]
-    small[:, row_width:] = numbers[...]
-
-    def weigh_share(route):
-        for block in range(route * share, (route + 1) * share):
-            touched = jnp.concatenate(
-                [
-                    estimate[owner_of[4 * block + part], pl.ds(sub_of[4 * block + part], 1), :]
-                    for part in range(4)
-                ],
-                axis=1,
-            )
-            shard[block], small[block : block + 1, :row_width] = weigh_block(
-                design[block],
-                touched,
-                observed[:, block : block + 1],
-                obs_type[:, block : block + 1],
-                sigma,
-            )
-
-    share = shard.shape[0] // len(routes)
+    _, block_rows, row_width = design.shape
+    per_owner, tile_width = estimate.shape[1:]
+    lane = lax.broadcasted_iota(jnp.int32, (1, tile_width), 1)
+    diagonal = lax.broadcasted_iota(
+        jnp.int32, (block_rows, block_rows), 0
+    ) == lax.broadcasted_iota(jnp.int32, (block_rows, block_rows), 1)
+
+    def upright(row):
+        return jnp.sum(jnp.where(diagonal, row, jnp.zeros_like(row)), axis=1, keepdims=True)
+
+    def weigh_one(block):
+        owners = [owner_of[block, part] for part in range(4)]
+        subs = [sub_of[block, part] for part in range(4)]
+        touched = jnp.concatenate(
+            [estimate[owner, pl.ds(sub, 1), :] for owner, sub in zip(owners, subs)], axis=1
+        )
+        numbers = jnp.zeros((1, tile_width), jnp.int32)
+        for part in range(4):
+            numbers = jnp.where(lane == part, owners[part] * per_owner + subs[part], numbers)
+        small[block : block + 1, row_width:] = numbers.astype(jnp.float32)
+        types = upright(obs_type[block : block + 1, :].astype(jnp.float32)).astype(jnp.int32)
+        rows, small[block : block + 1, :row_width] = weigh_block(
+            design[block], touched, upright(observed[block : block + 1, :]), types, sigma
+        )
+        shard[block * block_rows : (block + 1) * block_rows, :] = rows
+
+    unit = shard.shape[0] // sum(shares)
+    starts = [unit * sum(shares[:route]) for route in range(len(routes) + 1)]
 
     def copies(route, far, link, own=False, other=False):
         far_x, far_y, far_z = far
@@ -240,7 +247,7 @@
         chip = (arc + far_z) * 4 + from_y * 2 + from_x
         source = (arc + far_z) * 8 + at(from_y, from_x, 1 - core if other else core)
         number, device, _ = links[link]
-        rows = pl.ds(route * share, share)
+        rows = pl.ds(starts[route], starts[route + 1] - starts[route])
         arrive = 1 if other or link == "core" else 0
         made = [
             pltpu.make_async_remote_copy(
@@ -285,7 +292,10 @@
         def _(far=far, own=far == (0, 0, 0)):
             for route in range(len(routes)):
                 if own:
-                    weigh_share(route)
+                    for block in range(
+                        -(-starts[route] // block_rows), -(-starts[route + 1] // block_rows)
+                    ):
+                        weigh_one(block)
                 else:
                     for copy in copies(route, far, "x"):
                         copy.wait_recv()
@@ -323,24 +333,25 @@
         copy.wait()
 
 
-def spread_out(owner_of, sub_of, sigma, solution, numbers, design, observed, obs_type, n_arc):
+def spread_out(owner_of, sub_of, sigma, solution, design, observed, obs_type, n_arc):
     devices = n_arc * 8
     blocks, block_rows, row_width = design.shape
     hbm, vmem = pl.BlockSpec(memory_space=pl.ANY), pl.BlockSpec(memory_space=pltpu.VMEM)
     smem = pl.BlockSpec(memory_space=pltpu.SMEM)
     dma = pltpu.SemaphoreType.DMA
-    small = (blocks, row_width + numbers.shape[1])
+    shard = (blocks * block_rows, row_width)
+    small = (blocks, row_width + solution.shape[1])
     whole, whole_small = pl.pallas_call(
         functools.partial(spread_kernel, n_arc),
         out_shape=(
-            jax.ShapeDtypeStruct((devices, *design.shape), jnp.bfloat16),
+            jax.ShapeDtypeStruct((devices, *shard), jnp.bfloat16),
             jax.ShapeDtypeStruct((devices, *small), jnp.float32),
         ),
-        in_specs=[smem, smem, smem, vmem, vmem, vmem, vmem, vmem],
+        in_specs=[smem, smem, smem, vmem, vmem, vmem, vmem],
         out_specs=(hbm, hbm),
         scratch_shapes=[
             pltpu.VMEM((8, *solution.shape), jnp.float32),
-            pltpu.VMEM(design.shape, jnp.bfloat16),
+            pltpu.VMEM(shard, jnp.bfloat16),
             pltpu.VMEM(small, jnp.float32),
             dma((len(routes), n_arc * 4, 5)),
             dma((len(routes), n_arc * 4, 2)),
@@ -354,16 +365,7 @@
             collective_id=0, has_side_effects=True, vmem_limit_bytes=56 << 20
         ),
         name="spread",
-    )(
-        owner_of.reshape(-1),
-        sub_of.reshape(-1),
-        sigma,
-        solution,
-        numbers,
-        design,
-        observed.T,
-        obs_type.T,
-    )
+    )(owner_of, sub_of, sigma, solution, design, observed, obs_type)
     return whole.reshape(-1, block_rows, row_width), whole_small.reshape(-1, small[1])
 
 
@@ -409,15 +411,13 @@
     capacity = 2 * ((4 * blocks + n_owner - 1) // n_owner)
     everyone = ("arc", "tile")
     tile_ids = owner_of * per_owner + sub_of
-    by_route = n_owner == 8 and capacity >= blocks and blocks % len(routes) == 0
+    by_route = n_owner == 8 and capacity >= blocks and blocks * block_rows % 256 == 0
     if by_route:
-        numbers = jnp.pad(tile_ids.astype(jnp.float32), ((0, 0), (0, tile_width - 4)))
         items, pull = spread_out(
             owner_of,
             sub_of,
             sigma_table,
             solution.reshape(per_owner, tile_width),
-            numbers,
             design,
             observed,
             obs_type,

time: 194 us -> 189 us (0.974)
  local copies, waits for them, and re-layouts: 7.02 us -> 3.6 us
    unnamed x4 -> x2, local copies, waits for them, and re-layouts: 4.33 us -> 2.7 us
where the time goes in v3:
time: 189 us; the launch traced here: 188 us
  Pallas kernels  182 us (96%)
  local copies, waits for them, and re-layouts  3.6 us (2%)
  other arithmetic  2.47 us (1%)
    pallas_call x1, Pallas kernels, spread_out(): pl.pallas_call(functools.partial(spread_kernel, n_arc), out_shape=(jax.Sh...  139 us
    pallas_call x1, Pallas kernels, gram(): pl.pallas_call(functools.partial(gram_kernel, row_groups), grid_spec=pltp...  42.4 us

profile of v3, /device:TPU:0, one launch (start us, length us, event | category | flops | bytes accessed | tf_op | source)
XLA Modules:
  0.0 188.5 jit_solution(16299697005829867537)
XLA Ops:
  0.6 1.3 copy.12.owner_of
  2.0 1.3 copy.13.sub_of
  3.3 139.3 %spread.1 = (bf16[32,1024,512]{2,1,0:T(8,128)(2,1)}, f32[32,8,640]{2,1,0:T(8,128)}) custom-call(s32[8,4]{1,0:T(8,128)} %copy.12.owner_of, s32[8,4]{1,0:T(8,128)} %copy.13.sub_of, f32[8]{0:T(128)} %sigma.1, f32[12,128]{1,0:T(8,128)} %bitcast.14, bf16[8,128,512]{2,1,0:T(8,128)(2,1)} %design.1, f32[8,128]{1,0:T(8,128)} %observed.1, s32[8,128]{1,0:T(8,128)} %obs_type.1), custom_call_target="tpu_custom_call" | custom-call | tf_op jit(solution)/shard_map/spread/pallas_call | solution.py:344
  142.7 1.1 fusion.2
  143.8 0.1 fusion.5
  143.9 1.2 select_reduce_fusion
  145.2 0.1 copy.14
  145.3 0.7 reshape.81.table
  146.0 42.4 %gram.1 = (f32[3072,1536]{1,0:T(8,128)}, f32[12,128]{1,0:T(8,128)}) custom-call(s32[1536]{0:T(1024)} %reshape.81.table, bf16[256,128,512]{2,1,0:T(8,128)(2,1)} %bitcast.10, f32[256,640]{1,0:T(8,128)} %bitcast.13, f32[3072,1536]{1,0:T(8,128)} %prior.1), custom_call_target="tpu_custom_call" | custom-call | tf_op jit(solution)/shard_map/gram/pallas_call | solution.py:112
  (2 shorter events, 0.0 us)

commit v4 on v3

--- a/solution.py
+++ b/solution.py
@@ -55,18 +55,32 @@
     )(tile_ids, sigma, estimate, design, observed.T, obs_type.T)
 
 
-def gram_kernel(row_groups, table, items, pull, prior, normal, gradient, total, grad_total, sem):
+def gram_kernel(
+    row_groups, table, items, pull, prior, normal, gradient, total, grad_total, before, load_sem, sems
+):
     step = pl.program_id(0)
     chunk, _, row_width = items.shape
     tile_width = row_width // 4
     kept = normal.shape[0]
-    load = pltpu.make_async_copy(prior, total.at[pl.ds(0, kept)], sem)
+    load = pltpu.make_async_copy(prior, before, load_sem)
+
+    def slab(index):
+        return pl.ds(pl.multiple_of(index * tile_width, tile_width), tile_width)
+
+    def store(index):
+        return pltpu.make_async_copy(
+            total.at[slab(index)], normal.at[slab(index)], sems.at[index]
+        )
 
     @pl.when(step == 0)
     def _():
         load.start()
         grad_total[...] = jnp.zeros_like(grad_total)
-        load.wait()
+
+        @pl.loop(0, kept // tile_width)
+        def _(index):
+            total[slab(index), :] = jnp.zeros((tile_width, total.shape[1]), jnp.float32)
+
 
     fields = 2 + 2 * row_groups
     for item in range(chunk):
@@ -98,10 +112,18 @@
 
     @pl.when(step == pl.num_programs(0) - 1)
     def _():
-        store = pltpu.make_async_copy(total.at[pl.ds(0, kept)], normal, sem)
-        store.start()
+        load.wait()
+
+        @pl.loop(0, kept // tile_width)
+        def _(index):
+            total[slab(index), :] += before[slab(index), :]
+            store(index).start()
+
         gradient[...] = grad_total[: gradient.shape[0]]
-        store.wait()
+
+        @pl.loop(0, kept // tile_width)
+        def _(index):
+            store(index).wait()
 
 
 def gram(table, items, pull, prior, per_owner, row_groups, chunk):
@@ -126,7 +148,9 @@
             scratch_shapes=[
                 pltpu.VMEM((kept + tile_width, width), jnp.float32),
                 pltpu.VMEM((padded, tile_width), jnp.float32),
+                pltpu.VMEM(prior.shape, jnp.float32),
                 pltpu.SemaphoreType.DMA,
+                pltpu.SemaphoreType.DMA((kept // tile_width,)),
             ],
         ),
         out_shape=(
@@ -450,7 +474,7 @@
     table = item_table(
         tile_ids, lax.axis_index("arc"), lax.axis_index("tile"), per_owner, row_groups
     )
-    normal, gradient = gram(table, items, pull, prior, per_owner, row_groups, blocks)
+    normal, gradient = gram(table, items, pull, prior, per_owner, row_groups, 2 * blocks)
     return normal, gradient.reshape(-1)
 
 

time: 189 us -> 179 us (0.947)
  Pallas kernels: 182 us -> 172 us
    pallas_call x1, Pallas kernels: 42.4 us -> 32.5 us  [gram(): pl.pallas_call(functools.partial(gram_kernel, row_groups), grid_spec=pltp...]
where the time goes in v4:
time: 179 us
  Pallas kernels  172 us (96%)
  local copies, waits for them, and re-layouts  3.6 us (2%)
  other arithmetic  2.47 us (1%)
    pallas_call x1, Pallas kernels, spread_out(): pl.pallas_call(functools.partial(spread_kernel, n_arc), out_shape=(jax.Sh...  139 us
    pallas_call x1, Pallas kernels, gram(): pl.pallas_call(functools.partial(gram_kernel, row_groups), grid_spec=pltp...  32.5 us

profile of v4, /device:TPU:0, one launch (start us, length us, event | category | flops | bytes accessed | tf_op | source)
XLA Modules:
  0.0 178.6 jit_solution(16779544561330432967)
XLA Ops:
  0.6 1.3 copy.12.owner_of
  2.0 1.3 copy.13.sub_of
  3.3 139.3 %spread.1 = (bf16[32,1024,512]{2,1,0:T(8,128)(2,1)}, f32[32,8,640]{2,1,0:T(8,128)}) custom-call(s32[8,4]{1,0:T(8,128)} %copy.12.owner_of, s32[8,4]{1,0:T(8,128)} %copy.13.sub_of, f32[8]{0:T(128)} %sigma.1, f32[12,128]{1,0:T(8,128)} %bitcast.14, bf16[8,128,512]{2,1,0:T(8,128)(2,1)} %design.1, f32[8,128]{1,0:T(8,128)} %observed.1, s32[8,128]{1,0:T(8,128)} %obs_type.1), custom_call_target="tpu_custom_call" | custom-call | tf_op jit(solution)/shard_map/spread/pallas_call | solution.py:368
  142.7 1.1 fusion.2
  143.8 0.1 fusion.5
  143.9 1.2 select_reduce_fusion
  145.2 0.1 copy.14
  145.3 0.7 reshape.81.table
  146.0 32.5 %gram.1 = (f32[3072,1536]{1,0:T(8,128)}, f32[12,128]{1,0:T(8,128)}) custom-call(s32[1536]{0:T(1024)} %reshape.81.table, bf16[256,128,512]{2,1,0:T(8,128)(2,1)} %bitcast.10, f32[256,640]{1,0:T(8,128)} %bitcast.13, f32[3072,1536]{1,0:T(8,128)} %prior.1), custom_call_target="tpu_custom_call" | custom-call | tf_op jit(solution)/shard_map/gram/pallas_call | solution.py:134
  (2 shorter events, 0.0 us)
